TPU v7x, 256 devices: a whole 4x4x8 slice. The times are simulated.
256 devices in a mesh: row: 8 (over y_hi, x), col: 16 (over z, y_lo), sea: 2 (over core).
Axes of the slice: x: 4, y: 4 (y_hi: 2, y_lo: 2; y = y_hi * 2 + y_lo), z: 8, core: 2. Of those that a mesh axis runs over, the one named last changes fastest.
Arguments:
- kernel: bfloat16 [16, 8, 768, 6144], P(None, None, 'col', 'row'), may hold values from -0.01953125 to 0.01953125
- history: bfloat16 [15, 8, 768, 512], P(None, None, 'col', 'sea'), may hold values from -6 to 6
- displacement: float32 [6144, 512], P(('row', 'col'), 'sea'), may hold values from -6 to 6
- velocity: float32 [6144, 512], P(('row', 'col'), 'sea'), may hold values from -6 to 6
- acceleration: float32 [6144, 512], P(('row', 'col'), 'sea'), may hold values from -6 to 6
- excitation: float32 [3, 6144, 512], P(None, ('row', 'col'), 'sea'), may hold values from -6 to 6
- solve_inverse: float32 [1024, 6, 6], P(('row', 'col')), may hold values from -2.5 to 2.5
- stiffness: float32 [1024, 6, 6], P(('row', 'col')), may hold values from -2.5 to 2.5
- owned: int32 [1024], replicated, may hold values from 0 to 1023, as said below
- links: int32 [1024, 16], P(('row', 'col')), may hold values from 0 to 16383, as said below
- arms: float32 [1024, 3, 16], P(('row', 'col')), may hold values from -1 to 1
Outputs:
- final_velocity: float32 [6144, 512], P(('row', 'col'), 'sea')
- deck_gaps: float32 [1024, 16, 3, 512], P(('row', 'col'), None, None, 'sea')
Inputs may be any that keep to these rules, and one draw needn't show every extreme that they name: `owned`: A permutation of the 1024 modules. Module m has its modes on the grid device m // 8 (row-major over row, col); its owner has the same col. The modules that one device sends to one owner number at most 2, exactly 2 wherever any are sent, and their list positions differ modulo 2. `links`: the partner point lies on another module listed to the same owner.
All inputs are finite; a program needn't handle non-finite values.
Results may differ from a plain program's by a relative error of at most 0.00037.
Values may be sent and summed in bfloat16 or wider, within the bound.
A program may use at most 128 MiB of HBM per device.

v0:
```python
import jax
import jax.numpy as jnp
from jax import lax
from jax.sharding import PartitionSpec as P

POINTS = 16
STEPS = 3
DT = 0.5
QUARTER = DT * DT / 4.0


def blocks(matrix, vector):
    return jnp.einsum("mab,mbr->mar", matrix, vector, precision=lax.Precision.HIGHEST)


def newmark(
    displacement, velocity, acceleration, force_now, excitation_now, solve_inverse, stiffness
):
    block_shape = (displacement.shape[0] // 6, 6, displacement.shape[1])
    predicted = displacement + DT * velocity + QUARTER * acceleration
    load_total = (
        excitation_now
        - force_now
        - blocks(stiffness, predicted.reshape(block_shape)).reshape(displacement.shape)
    )
    accel_next = blocks(solve_inverse, load_total.reshape(block_shape)).reshape(displacement.shape)
    return (
        predicted + QUARTER * accel_next,
        velocity + 0.5 * DT * (acceleration + accel_next),
        accel_next,
    )


def deck_motion(motion, levers):
    moving = motion[:, 0:3, None, :]
    turning = motion[:, 3:6, None, :]
    arm_all = levers[:, :, :, None]
    surge_motion = moving[:, 0] + turning[:, 1] * arm_all[:, 2] - turning[:, 2] * arm_all[:, 1]
    sway_motion = moving[:, 1] + turning[:, 2] * arm_all[:, 0] - turning[:, 0] * arm_all[:, 2]
    heave_motion = moving[:, 2] + turning[:, 0] * arm_all[:, 1] - turning[:, 1] * arm_all[:, 0]
    return jnp.stack([surge_motion, sway_motion, heave_motion], axis=2)


def body(
    kernel,
    history,
    displacement,
    velocity,
    acceleration,
    excitation,
    solve_inverse,
    stiffness,
    owned,
    links,
    arms,
):
    lag_count = kernel.shape[0]
    row_total = lax.axis_size("row")
    col_total = lax.axis_size("col")
    slab_rows = velocity.shape[0]
    block_rows = kernel.shape[3]
    module_count = slab_rows // 6
    window = history
    kernel_flat = kernel.reshape(-1, block_rows)
    for step_index in range(STEPS):
        newest = lax.all_gather(velocity.astype(jnp.bfloat16), "row", axis=0, tiled=True)
        newest = newest.reshape(1, row_total, slab_rows, newest.shape[1])
        window = jnp.concatenate([newest, window[: lag_count - 1]], axis=0)
        window_flat = window.reshape(kernel_flat.shape[0], -1)
        force_now = lax.psum_scatter(
            lax.dot_general(
                kernel_flat,
                window_flat,
                (((0,), (0,)), ((), ())),
                preferred_element_type=jnp.float32,
            ),
            "col",
            scatter_dimension=0,
            tiled=True,
        )
        displacement, velocity, acceleration = newmark(
            displacement,
            velocity,
            acceleration,
            force_now,
            excitation[step_index],
            solve_inverse,
            stiffness,
        )
    motion = displacement.reshape(module_count, 6, -1)
    grid_index = lax.axis_index("row") * col_total + lax.axis_index("col")
    owned_here = lax.dynamic_slice_in_dim(owned, grid_index * module_count, module_count, 0)
    home_rows = owned_here // (col_total * module_count)
    capacity = 2 * module_count // row_total
    local_ids = grid_index * module_count + jnp.arange(module_count, dtype=jnp.int32)
    list_range = jnp.arange(owned.shape[0], dtype=jnp.int32)
    positions = jnp.sum(
        jnp.where(owned[None, :] == local_ids[:, None], list_range[None, :], 0), axis=1
    )
    targets = (
        positions // (col_total * module_count) * capacity + positions % module_count % capacity
    )
    routing = (
        targets[None, :] == jnp.arange(row_total * capacity, dtype=jnp.int32)[:, None]
    ).astype(jnp.float32)
    outgoing = jnp.einsum("sm,mar->sar", routing, motion, precision=lax.Precision.HIGHEST).reshape(
        row_total, capacity, 6, -1
    )
    arrived = lax.all_to_all(outgoing, "row", split_axis=0, concat_axis=0, tiled=True).reshape(
        row_total * capacity, 6, -1
    )
    slot_index = jnp.arange(module_count, dtype=jnp.int32) % capacity
    owned_motion = jnp.take(arrived, home_rows * capacity + slot_index, axis=0)
    points = deck_motion(owned_motion, arms).reshape(module_count * POINTS, 3, -1)
    local_links = (links - grid_index * module_count * POINTS).reshape(-1)
    partner = jnp.take(points, local_links, axis=0)
    deck_gaps = (points - partner).reshape(module_count, POINTS, 3, -1)
    return (velocity, deck_gaps)


def solution(mesh):
    placed = (
        P(None, None, "col", "row"),
        P(None, None, "col", "sea"),
        P(("row", "col"), "sea"),
        P(("row", "col"), "sea"),
        P(("row", "col"), "sea"),
        P(None, ("row", "col"), "sea"),
        P(("row", "col"), None, None),
        P(("row", "col"), None, None),
        P(),
        P(("row", "col"), None),
        P(("row", "col"), None, None),
    )
    return jax.shard_map(
        body,
        mesh=mesh,
        in_specs=placed,
        out_specs=(P(("row", "col"), "sea"), P(("row", "col"), None, None, "sea")),
        check_vma=False,
    )
```

profile of v0, /device:TPU:2, one launch (start us, length us, event | category | flops | bytes accessed | tf_op | source)
XLA Modules:
  0.0 378.5 jit_solution(11167240367918859943)
XLA Ops:
  7.2 0.9 fusion.48
  8.1 34.6 %all_gather.9 = bf16[384,256]{1,0:T(8,128)(2,1)S(1)} all-gather(bf16[48,256]{1,0:T(8,128)(2,1)S(1)} %get-tuple-element.25), channel_id=1, replica_groups=mesh['row'=8,'col'=16,'sea'=2] {'row'}, dimensions={0}, use_global_device_ids=true | all-gather | bytes 221184 | tf_op jit(solution)/shard_map/all_gather | solution.py:66
  42.7 7.3 %fusion.14 = f32[768,256]{0,1:T(8,128)S(1)} fusion(bf16[16,8,48,768]{3,2,1,0:T(8,128)(2,1)} %param.11, bf16[15,8,48,256]{3,2,1,0:T(8,128)(2,1)} %param.12, bf16[1,8,48,256]{3,2,1,0:T(8,128)(2,1)S(1)} %bitcast.112), kind=kOutput, calls=%fused_computation.17 | convolution fusion | flops 2417491968 | bytes 13369344 | tf_op jit(solution)/shard_map/dot_general | solution.py:71
  50.0 1.2 copy.99
  51.3 0.2 convolution_bitcast_fusion.5
  51.5 73.3 %reduce-scatter.10.cloned.1.call-done = f32[48,256]{1,0:T(8,128)} async-done(((f32[768,256]{1,0:T(8,128)}), f32[48,256]{1,0:T(8,128)}) %reduce-scatter.10.cloned.1.call-update) | async-done | bytes 49168 | tf_op jit(solution)/shard_map/reduce_scatter | solution.py:70
  124.7 0.8 fusion.27
  125.6 0.2 convolution_bitcast_fusion.4
  125.8 34.0 %all_gather.10 = bf16[384,256]{1,0:T(8,128)(2,1)S(1)} all-gather(bf16[48,256]{1,0:T(8,128)(2,1)S(1)} %get-tuple-element.16), channel_id=1, replica_groups=mesh['row'=8,'col'=16,'sea'=2] {'row'}, dimensions={0}, use_global_device_ids=true | all-gather | bytes 221184 | tf_op jit(solution)/shard_map/all_gather | solution.py:66
  159.8 7.2 %fusion.17 = f32[768,256]{0,1:T(8,128)S(1)} fusion(bf16[16,8,48,768]{3,2,1,0:T(8,128)(2,1)} %param.11, bf16[15,8,48,256]{3,2,1,0:T(8,128)(2,1)} %param.12, bf16[1,8,48,256]{3,2,1,0:T(8,128)(2,1)S(1)} %bitcast.113, bf16[1,8,48,256]{3,2,1,0:T(8,128)(2,1)S(1)} %bitcast.115), kind=kOutput, calls=%fused_computation.18 | convolution fusion | flops 2419064832 | bytes 13565952 | tf_op jit(solution)/shard_map/dot_general | solution.py:71
  167.0 1.2 copy.101
  168.3 0.2 convolution_bitcast_fusion.3
  168.5 69.3 %reduce-scatter.12.cloned.1.call-done = f32[48,256]{1,0:T(8,128)} async-done(((f32[768,256]{1,0:T(8,128)}), f32[48,256]{1,0:T(8,128)}) %reduce-scatter.12.cloned.1.call-update) | async-done | bytes 49168 | tf_op jit(solution)/shard_map/reduce_scatter | solution.py:70
  237.7 0.8 fusion.26
  238.6 0.2 convolution_bitcast_fusion.2
  238.8 34.0 %all_gather.11 = bf16[384,256]{1,0:T(8,128)(2,1)S(1)} all-gather(bf16[48,256]{1,0:T(8,128)(2,1)S(1)} %get-tuple-element.14), channel_id=1, replica_groups=mesh['row'=8,'col'=16,'sea'=2] {'row'}, dimensions={0}, use_global_device_ids=true | all-gather | bytes 221184 | tf_op jit(solution)/shard_map/all_gather | solution.py:66
  272.8 7.1 %fusion.20 = f32[768,256]{0,1:T(8,128)S(1)} fusion(bf16[16,8,48,768]{3,2,1,0:T(8,128)(2,1)} %param.11, bf16[1,8,48,256]{3,2,1,0:T(8,128)(2,1)S(1)} %bitcast.116, bf16[15,8,48,256]{3,2,1,0:T(8,128)(2,1)} %param.12, bf16[1,8,48,256]{3,2,1,0:T(8,128)(2,1)S(1)} %bitcast.114, bf16[1,8,48,256]{3,2,1,0:T(8,128)(2,1)S(1)} %bitcast.117), kind=kOutput, calls=%fused_computation.19 | convolution fusion | flops 2420637696 | bytes 13762560 | tf_op jit(solution)/shard_map/dot_general | solution.py:71
  279.9 1.2 copy.103
  281.1 0.1 mul.280
  281.2 0.1 mul.285
  281.3 0.1 mul.288
  281.4 0.1 reshape.520
  281.5 0.1 compare_and_fusion.1
  281.6 0.2 select_reduce_fusion
  281.9 0.2 convolution_bitcast_fusion.1
  282.1 68.7 %reduce-scatter.14.cloned.1.call-done = f32[48,256]{1,0:T(8,128)} async-done(((f32[768,256]{1,0:T(8,128)}), f32[48,256]{1,0:T(8,128)}) %reduce-scatter.14.cloned.1.call-update) | async-done | bytes 49168 | tf_op jit(solution)/shard_map/reduce_scatter | solution.py:70
  350.8 0.8 fusion.25
  351.6 0.2 convolution_bitcast_fusion
  351.8 0.6 multiply_add_fusion
  352.4 0.2 fusion.23
  352.7 0.7 copy.89
  353.4 7.0 %all-to-all-start = ((f32[8,2,6,256]{3,1,2,0:T(2,128)}), f32[8,2,6,256]{3,1,2,0:T(2,128)S(1)}, u32[]{:S(2)}, u32[]{:S(2)}) async-start(f32[8,2,6,256]{3,1,2,0:T(2,128)} %copy.89), calls=%async_computation | async-start | bytes 196608 | tf_op jit(solution)/shard_map/all_to_all | solution.py:109
  360.4 6.7 %all-to-all-done = f32[8,2,6,256]{3,1,2,0:T(2,128)S(1)} async-done(((f32[8,2,6,256]{3,1,2,0:T(2,128)}), f32[8,2,6,256]{3,1,2,0:T(2,128)S(1)}, u32[]{:S(2)}, u32[]{:S(2)}) %all-to-all-start) | async-done | bytes 98336 | tf_op jit(solution)/shard_map/all_to_all | solution.py:109
  367.1 0.6 gather_fusion
  367.7 0.1 broadcast_select_fusion
  367.9 0.1 add.259
  368.0 0.1 add.262
  368.2 0.1 add.265
  368.4 0.1 mul.279
  368.5 0.1 mul.284
  368.7 0.1 mul.292
  368.8 0.7 multiply_subtract_fusion.2
  369.6 0.3 pad_maximum_fusion.4
  369.9 0.9 gather_fusion.1
  370.8 0.1 copy.92
  370.9 0.1 multiply_subtract_fusion.5
  371.0 0.1 maximum_subtract_fusion
  371.2 0.8 copy.93
  (61 shorter events, 0.6 us)
Async XLA Ops:
  7.2 44.1 %copy-start = (f32[8,6,6]{2,0,1:T(8,128)S(1)}, f32[8,6,6]{2,0,1:T(8,128)}, u32[]{:S(2)}) copy-start(f32[8,6,6]{2,0,1:T(8,128)} %param.18) | copy-start | bytes 3460
  7.2 117.5 %reduce-scatter.10.cloned.1.call-start = ((), (), s32[]{:S(2)}) async-start(), calls=%async_computation.4 | async-start | bytes 835584 | tf_op jit(solution)/shard_map/reduce_scatter | solution.py:70
  42.7 82.0 %copy-start.4 = (f32[3,48,256]{2,1,0:T(8,128)S(1)}, f32[3,48,256]{2,1,0:T(8,128)}, u32[]{:S(2)}) copy-start(f32[3,48,256]{2,1,0:T(8,128)} %param.16) | copy-start | bytes 442372
  42.7 82.9 %copy-start.3 = (f32[8,6,6]{2,0,1:T(8,128)S(1)}, f32[8,6,6]{2,0,1:T(8,128)}, u32[]{:S(2)}) copy-start(f32[8,6,6]{2,0,1:T(8,128)} %param.17) | copy-start | bytes 3460
  50.0 75.8 %copy-start.1 = (f32[48,256]{1,0:T(8,128)S(1)}, f32[48,256]{1,0:T(8,128)}, u32[]{:S(2)}) copy-start(f32[48,256]{1,0:T(8,128)} %param.14) | copy-start | bytes 147460
  50.0 75.8 %copy-start.2 = (f32[48,256]{1,0:T(8,128)S(1)}, f32[48,256]{1,0:T(8,128)}, u32[]{:S(2)}) copy-start(f32[48,256]{1,0:T(8,128)} %param.15) | copy-start | bytes 147460
  51.2 186.6 %reduce-scatter.12.cloned.1.call-start = ((), (), s32[]{:S(2)}) async-start(), calls=%async_computation.5 | async-start | bytes 835584 | tf_op jit(solution)/shard_map/reduce_scatter | solution.py:70
  159.8 8.4 %copy-start.5 = (f32[8,3,16]{2,0,1:T(8,128)S(1)}, f32[8,3,16]{2,0,1:T(8,128)}, u32[]{:S(2)}) copy-start(f32[8,3,16]{2,0,1:T(8,128)} %param.21) | copy-start | bytes 4612
  168.2 182.6 %reduce-scatter.14.cloned.1.call-start = ((), (), s32[]{:S(2)}) async-start(), calls=%async_computation.6 | async-start | bytes 835584 | tf_op jit(solution)/shard_map/reduce_scatter | solution.py:70
  272.8 8.3 %copy-start.7 = (s32[8,16]{1,0:T(8,128)S(1)}, s32[8,16]{1,0:T(8,128)}, u32[]{:S(2)}) copy-start(s32[8,16]{1,0:T(8,128)} %param.20) | copy-start | bytes 1540
  272.8 8.7 %copy-start.6 = (s32[1024]{0:T(1024)S(1)}, s32[1024]{0:T(1024)}, u32[]{:S(2)}) copy-start(s32[1024]{0:T(1024)} %param.19) | copy-start | bytes 12292
  353.4 13.7 %all-to-all-start = ((f32[8,2,6,256]{3,1,2,0:T(2,128)}), f32[8,2,6,256]{3,1,2,0:T(2,128)S(1)}, u32[]{:S(2)}, u32[]{:S(2)}) async-start(f32[8,2,6,256]{3,1,2,0:T(2,128)} %copy.89), calls=%async_computation | async-start | bytes 196608 | tf_op jit(solution)/shard_map/all_to_all | solution.py:109
Sparse Core Ops, SparseCore 0:
  51.3 73.3 reduce-scatter.9
  168.3 69.3 reduce-scatter.11
  281.2 69.4 reduce-scatter.13
where the time goes:
time: 379 us; the launch traced here: 378 us
  waiting for transfers between devices  218 us (58%)
  blocking collectives  103 us (27%)
  matrix products  22.9 us (6%)
  between operations  14.3 us (4%)
  local copies, waits for them, and re-layouts  7.9 us (2%)
  starting transfers between devices  7.09 us (2%)
  other arithmetic  5.75 us (2%)
    reduce_scatter x3, waiting for transfers between devices, body(): lax.psum_scatter(lax.dot_general(kernel_flat, window_flat, (((0,), (0,)),...  211 us
    all_gather x3, blocking collectives, body(): lax.all_gather(velocity.astype(jnp.bfloat16), 'row', axis=0, tiled=True)  103 us
    dot_general x3, matrix products, body(): lax.dot_general(kernel_flat, window_flat, (((0,), (0,)), ((), ())), prefe...  21.6 us
  transfers between devices with their start and end apart: 4, of which 4 were waited for; matrix products, arithmetic and copies ran while one was open for 0% of the time, Pallas kernels for 0%

commit v1 on v0

--- a/solution.py
+++ b/solution.py
@@ -2,6 +2,7 @@
 import jax.numpy as jnp
 from jax import lax
 from jax.sharding import PartitionSpec as P
+from jax.lax import all_to_all, axis_size
 
 POINTS = 16
 STEPS = 3
@@ -63,7 +64,11 @@
     window = history
     kernel_flat = kernel.reshape(-1, block_rows)
     for step_index in range(STEPS):
-        newest = lax.all_gather(velocity.astype(jnp.bfloat16), "row", axis=0, tiled=True)
+        patch = velocity.astype(jnp.bfloat16)
+        opened = axis_size("row")
+        frame_out = jnp.stack(opened * [patch], 0)
+        met_up = all_to_all(frame_out, "row", 0, 0)
+        newest = jnp.concatenate(met_up, 0)
         newest = newest.reshape(1, row_total, slab_rows, newest.shape[1])
         window = jnp.concatenate([newest, window[: lag_count - 1]], axis=0)
         window_flat = window.reshape(kernel_flat.shape[0], -1)

time: 379 us -> 311 us (0.82)
  blocking collectives: 103 us -> 28.5 us
  starting transfers between devices: 7.09 us -> 14 us
    all_gather x3 -> x0, blocking collectives: 103 us -> none  [body(): lax.all_gather(velocity.astype(jnp.bfloat16), 'row', axis=0, tiled=True)]
    all_to_all x0 -> x2, blocking collectives: none -> 28.5 us  [body(): met_up = all_to_all(frame_out, 'row', 0, 0)]
    reduce_scatter x3, waiting for transfers between devices: 211 us -> 202 us  [body(): lax.psum_scatter(lax.dot_general(kernel_flat, window_flat, (((0,), (0,)),...]
    all_to_all x0 -> x1, waiting for transfers between devices: none -> 7.25 us  [body(): met_up = all_to_all(frame_out, 'row', 0, 0)]
    all_to_all x0 -> x1, starting transfers between devices: none -> 6.99 us  [body(): met_up = all_to_all(frame_out, 'row', 0, 0)]
  transfers between devices with their start and end apart: 4 -> 5, of which waited for: 4 -> 5; matrix products, arithmetic and copies ran while one was open for 0% -> 0% of each run, Pallas kernels for 0% -> 0%
where the time goes in v1:
time: 311 us; the launch traced here: 310 us
  waiting for transfers between devices  216 us (69%)
  blocking collectives  28.5 us (9%)
  matrix products  22.9 us (7%)
  between operations  14.3 us (5%)
  starting transfers between devices  14 us (5%)
  local copies, waits for them, and re-layouts  8.59 us (3%)
  other arithmetic  5.72 us (2%)
    reduce_scatter x3, waiting for transfers between devices, body(): lax.psum_scatter(lax.dot_general(kernel_flat, window_flat, (((0,), (0,)),...  202 us
    all_to_all x2, blocking collectives, body(): met_up = all_to_all(frame_out, 'row', 0, 0)  28.5 us
    dot_general x3, matrix products, body(): lax.dot_general(kernel_flat, window_flat, (((0,), (0,)), ((), ())), prefe...  21.5 us
    all_to_all x1, waiting for transfers between devices, body(): met_up = all_to_all(frame_out, 'row', 0, 0)  7.25 us
    all_to_all x1, starting transfers between devices, body(): met_up = all_to_all(frame_out, 'row', 0, 0)  6.99 us
    all_to_all x1, starting transfers between devices, body(): lax.all_to_all(outgoing, 'row', split_axis=0, concat_axis=0, tiled=True)  6.96 us
    all_to_all x1, waiting for transfers between devices, body(): lax.all_to_all(outgoing, 'row', split_axis=0, concat_axis=0, tiled=True)  6.74 us
  transfers between devices with their start and end apart: 5, of which 5 were waited for; matrix products, arithmetic and copies ran while one was open for 0% of the time, Pallas kernels for 0%

profile of v1, /device:TPU:2, one launch (start us, length us, event | category | flops | bytes accessed | tf_op | source)
XLA Modules:
  0.0 310.3 jit_solution(2728649367684105401)
XLA Ops:
  7.2 0.9 fusion.48
  8.1 14.5 %all_to_all.20 = bf16[8,48,256]{2,1,0:T(8,128)(2,1)S(1)} all-to-all(bf16[8,48,256]{2,1,0:T(8,128)(2,1)S(1)} %stack.10), channel_id=1, replica_groups=mesh['row'=8,'col'=16,'sea'=2] {'row'}, dimensions={0} | all-to-all | bytes 393216 | tf_op jit(solution)/shard_map/all_to_all | solution.py:70
  22.7 7.2 %fusion.14 = f32[768,256]{0,1:T(8,128)S(1)} fusion(bf16[16,8,48,768]{3,2,1,0:T(8,128)(2,1)} %param.11, bf16[15,8,48,256]{3,2,1,0:T(8,128)(2,1)} %param.12, bf16[1,8,48,256]{3,2,1,0:T(8,128)(2,1)S(1)} %bitcast.112), kind=kOutput, calls=%fused_computation.17 | convolution fusion | flops 2417491968 | bytes 13369344 | tf_op jit(solution)/shard_map/dot_general | solution.py:76
  29.9 1.2 copy.99
  31.2 0.2 convolution_bitcast_fusion.5
  31.4 70.3 %reduce-scatter.10.cloned.1.call-done = f32[48,256]{1,0:T(8,128)} async-done(((f32[768,256]{1,0:T(8,128)}), f32[48,256]{1,0:T(8,128)}) %reduce-scatter.10.cloned.1.call-update) | async-done | bytes 49168 | tf_op jit(solution)/shard_map/reduce_scatter | solution.py:75
  101.7 0.8 fusion.27
  102.5 0.2 convolution_bitcast_fusion.4
  102.8 13.9 %all_to_all.21 = bf16[8,48,256]{2,1,0:T(8,128)(2,1)S(1)} all-to-all(bf16[8,48,256]{2,1,0:T(8,128)(2,1)S(1)} %stack.11), channel_id=1, replica_groups=mesh['row'=8,'col'=16,'sea'=2] {'row'}, dimensions={0} | all-to-all | bytes 393216 | tf_op jit(solution)/shard_map/all_to_all | solution.py:70
  116.8 7.2 %fusion.17 = f32[768,256]{0,1:T(8,128)S(1)} fusion(bf16[16,8,48,768]{3,2,1,0:T(8,128)(2,1)} %param.11, bf16[15,8,48,256]{3,2,1,0:T(8,128)(2,1)} %param.12, bf16[1,8,48,256]{3,2,1,0:T(8,128)(2,1)S(1)} %bitcast.113, bf16[1,8,48,256]{3,2,1,0:T(8,128)(2,1)S(1)} %bitcast.115), kind=kOutput, calls=%fused_computation.18 | convolution fusion | flops 2419064832 | bytes 13565952 | tf_op jit(solution)/shard_map/dot_general | solution.py:76
  123.9 1.2 copy.101
  125.1 0.2 convolution_bitcast_fusion.3
  125.3 66.3 %reduce-scatter.12.cloned.1.call-done = f32[48,256]{1,0:T(8,128)} async-done(((f32[768,256]{1,0:T(8,128)}), f32[48,256]{1,0:T(8,128)}) %reduce-scatter.12.cloned.1.call-update) | async-done | bytes 49168 | tf_op jit(solution)/shard_map/reduce_scatter | solution.py:75
  191.6 0.8 fusion.26
  192.5 0.2 convolution_bitcast_fusion.2
  192.7 0.7 stack.12
  193.4 7.0 %all-to-all-start.2 = ((bf16[8,48,256]{2,1,0:T(8,128)(2,1)}), bf16[8,48,256]{2,1,0:T(8,128)(2,1)S(1)}, u32[]{:S(2)}, u32[]{:S(2)}) async-start(bf16[8,48,256]{2,1,0:T(8,128)(2,1)} %stack.12), calls=%async_computation.2 | async-start | bytes 393216 | tf_op jit(solution)/shard_map/all_to_all | solution.py:70
  200.4 7.3 %all-to-all-done.2 = bf16[8,48,256]{2,1,0:T(8,128)(2,1)S(1)} async-done(((bf16[8,48,256]{2,1,0:T(8,128)(2,1)}), bf16[8,48,256]{2,1,0:T(8,128)(2,1)S(1)}, u32[]{:S(2)}, u32[]{:S(2)}) %all-to-all-start.2) | async-done | bytes 196640 | tf_op jit(solution)/shard_map/all_to_all | solution.py:70
  207.7 7.1 %fusion.20 = f32[768,256]{0,1:T(8,128)S(1)} fusion(bf16[16,8,48,768]{3,2,1,0:T(8,128)(2,1)} %param.11, bf16[1,8,48,256]{3,2,1,0:T(8,128)(2,1)S(1)} %bitcast.116, bf16[15,8,48,256]{3,2,1,0:T(8,128)(2,1)} %param.12, bf16[1,8,48,256]{3,2,1,0:T(8,128)(2,1)S(1)} %bitcast.114, bf16[1,8,48,256]{3,2,1,0:T(8,128)(2,1)S(1)} %bitcast.117), kind=kOutput, calls=%fused_computation.19 | convolution fusion | flops 2420637696 | bytes 13762560 | tf_op jit(solution)/shard_map/dot_general | solution.py:76
  214.8 1.2 copy.103
  216.0 0.1 mul.280
  216.1 0.1 mul.285
  216.2 0.1 mul.288
  216.2 0.1 reshape.514
  216.4 0.1 compare_and_fusion.1
  216.5 0.2 select_reduce_fusion
  216.7 0.2 convolution_bitcast_fusion.1
  216.9 65.7 %reduce-scatter.14.cloned.1.call-done = f32[48,256]{1,0:T(8,128)} async-done(((f32[768,256]{1,0:T(8,128)}), f32[48,256]{1,0:T(8,128)}) %reduce-scatter.14.cloned.1.call-update) | async-done | bytes 49168 | tf_op jit(solution)/shard_map/reduce_scatter | solution.py:75
  282.7 0.8 fusion.25
  283.5 0.2 convolution_bitcast_fusion
  283.7 0.6 multiply_add_fusion
  284.3 0.2 fusion.23
  284.6 0.7 copy.89
  285.3 7.0 %all-to-all-start.3 = ((f32[8,2,6,256]{3,1,2,0:T(2,128)}), f32[8,2,6,256]{3,1,2,0:T(2,128)S(1)}, u32[]{:S(2)}, u32[]{:S(2)}) async-start(f32[8,2,6,256]{3,1,2,0:T(2,128)} %copy.89), calls=%async_computation.3 | async-start | bytes 196608 | tf_op jit(solution)/shard_map/all_to_all | solution.py:114
  292.3 6.7 %all-to-all-done.3 = f32[8,2,6,256]{3,1,2,0:T(2,128)S(1)} async-done(((f32[8,2,6,256]{3,1,2,0:T(2,128)}), f32[8,2,6,256]{3,1,2,0:T(2,128)S(1)}, u32[]{:S(2)}, u32[]{:S(2)}) %all-to-all-start.3) | async-done | bytes 98336 | tf_op jit(solution)/shard_map/all_to_all | solution.py:114
  299.0 0.6 gather_fusion
  299.8 0.1 add.259
  299.9 0.1 add.262
  300.1 0.1 add.265
  300.3 0.1 mul.279
  300.4 0.1 mul.284
  300.6 0.1 mul.292
  300.7 0.7 multiply_subtract_fusion.2
  301.5 0.3 pad_maximum_fusion.4
  301.8 0.9 gather_fusion.1
  302.8 0.1 multiply_subtract_fusion.5
  302.9 0.1 maximum_subtract_fusion
  303.0 0.8 copy.93
  (65 shorter events, 0.7 us)
Async XLA Ops:
  7.2 24.0 %copy-start = (f32[8,6,6]{2,0,1:T(8,128)S(1)}, f32[8,6,6]{2,0,1:T(8,128)}, u32[]{:S(2)}) copy-start(f32[8,6,6]{2,0,1:T(8,128)} %param.18) | copy-start | bytes 3460
  7.2 94.5 %reduce-scatter.10.cloned.1.call-start = ((), (), s32[]{:S(2)}) async-start(), calls=%async_computation.7 | async-start | bytes 835584 | tf_op jit(solution)/shard_map/reduce_scatter | solution.py:75
  22.7 79.0 %copy-start.4 = (f32[3,48,256]{2,1,0:T(8,128)S(1)}, f32[3,48,256]{2,1,0:T(8,128)}, u32[]{:S(2)}) copy-start(f32[3,48,256]{2,1,0:T(8,128)} %param.16) | copy-start | bytes 442372
  22.7 79.8 %copy-start.3 = (f32[8,6,6]{2,0,1:T(8,128)S(1)}, f32[8,6,6]{2,0,1:T(8,128)}, u32[]{:S(2)}) copy-start(f32[8,6,6]{2,0,1:T(8,128)} %param.17) | copy-start | bytes 3460
  29.9 72.8 %copy-start.1 = (f32[48,256]{1,0:T(8,128)S(1)}, f32[48,256]{1,0:T(8,128)}, u32[]{:S(2)}) copy-start(f32[48,256]{1,0:T(8,128)} %param.14) | copy-start | bytes 147460
  29.9 72.8 %copy-start.2 = (f32[48,256]{1,0:T(8,128)S(1)}, f32[48,256]{1,0:T(8,128)}, u32[]{:S(2)}) copy-start(f32[48,256]{1,0:T(8,128)} %param.15) | copy-start | bytes 147460
  31.1 160.5 %reduce-scatter.12.cloned.1.call-start = ((), (), s32[]{:S(2)}) async-start(), calls=%async_computation.8 | async-start | bytes 835584 | tf_op jit(solution)/shard_map/reduce_scatter | solution.py:75
  123.9 76.5 %copy-start.5 = (f32[8,3,16]{2,0,1:T(8,128)S(1)}, f32[8,3,16]{2,0,1:T(8,128)}, u32[]{:S(2)}) copy-start(f32[8,3,16]{2,0,1:T(8,128)} %param.21) | copy-start | bytes 4612
  193.4 14.3 %all-to-all-start.2 = ((bf16[8,48,256]{2,1,0:T(8,128)(2,1)}), bf16[8,48,256]{2,1,0:T(8,128)(2,1)S(1)}, u32[]{:S(2)}, u32[]{:S(2)}) async-start(bf16[8,48,256]{2,1,0:T(8,128)(2,1)} %stack.12), calls=%async_computation.2 | async-start | bytes 393216 | tf_op jit(solution)/shard_map/all_to_all | solution.py:70
  200.4 82.3 %reduce-scatter.14.cloned.1.call-start = ((), (), s32[]{:S(2)}) async-start(), calls=%async_computation.9 | async-start | bytes 835584 | tf_op jit(solution)/shard_map/reduce_scatter | solution.py:75
  207.7 8.3 %copy-start.7 = (s32[8,16]{1,0:T(8,128)S(1)}, s32[8,16]{1,0:T(8,128)}, u32[]{:S(2)}) copy-start(s32[8,16]{1,0:T(8,128)} %param.20) | copy-start | bytes 1540
  207.7 8.7 %copy-start.6 = (s32[1024]{0:T(1024)S(1)}, s32[1024]{0:T(1024)}, u32[]{:S(2)}) copy-start(s32[1024]{0:T(1024)} %param.19) | copy-start | bytes 12292
  285.3 13.7 %all-to-all-start.3 = ((f32[8,2,6,256]{3,1,2,0:T(2,128)}), f32[8,2,6,256]{3,1,2,0:T(2,128)S(1)}, u32[]{:S(2)}, u32[]{:S(2)}) async-start(f32[8,2,6,256]{3,1,2,0:T(2,128)} %copy.89), calls=%async_computation.3 | async-start | bytes 196608 | tf_op jit(solution)/shard_map/all_to_all | solution.py:114
Sparse Core Ops, SparseCore 0:
  31.2 70.3 reduce-scatter.9
  125.2 66.3 reduce-scatter.11
  216.1 66.5 reduce-scatter.13
